TPU v7x, 32 devices: a whole 2x2x4 slice. The times are simulated.
32 devices in a mesh: grp: 2 (over y), tp: 4 (over z), dp: 4 (over x, core).
Axes of the slice: x: 2, y: 2, z: 4, core: 2. Of those that a mesh axis runs over, the one named last changes fastest.
Arguments:
- layer_inputs: bfloat16 [16384, 8192], P(('grp', 'dp'), 'tp'), parts along dimension 0, may hold values from -6 to 6
- out_grads: bfloat16 [16384, 28672], P(('grp', 'dp'), 'tp'), parts along dimension 0, may hold values from -6 to 6
- doc_ids: int32 [8, 2048], P(('grp', 'dp')), parts along dimension 0, may hold values from 0 to 15, never falling along the last dimension, each value on 1 to 256 neighbouring positions
- proj_in: bfloat16 [8192, 64], P('tp'), may hold values from -0.0625 to 0.0625
- proj_out: bfloat16 [28672, 64], P('tp'), may hold values from -0.03125 to 0.03125
- query_feats: bfloat16 [4096, 1024], P('tp'), may hold values from -0.0078125 to 0.0078125
Outputs:
- scores: float32 [128, 1024], P(('grp', 'dp'), 'tp'), parts along dimension 0
There are 2 independent parts, one for each index of `grp`. A program takes and returns all parts, laid end to end along the dimension named above; an argument that names none is the same for every part. Nothing has to cross between parts.
Inputs may be any that keep to these rules, and one draw needn't show every extreme that they name: `doc_ids`: each row is non-decreasing; every label appears, on at most 256 tokens.
All inputs are finite; a program needn't handle non-finite values.
Results may differ from a plain program's by a relative error of at most 0.0049.
Values may be sent and summed in bfloat16 or wider, within the bound.
A program may use at most 128 MiB of HBM per device.

v0:
```python
import jax
import jax.numpy as jnp
from jax import lax
from jax.sharding import PartitionSpec as P

PI = 64
PO = 64
DOCS_DEV = 16


def doc_features(labels, in_proj, out_cols):
    tok_rows = in_proj.shape[0]
    docs = jnp.arange(DOCS_DEV, dtype=jnp.int32)
    onehot = (labels[:, None] == docs[None, :]).astype(jnp.bfloat16)
    spread = (onehot[:, :, None] * in_proj[:, None, :]).reshape(tok_rows, DOCS_DEV * PI)
    feats = jnp.einsum("tk,tj->kj", spread, out_cols, preferred_element_type=jnp.float32)
    cols = out_cols.shape[1]
    return feats.reshape(DOCS_DEV, PI, cols).transpose(0, 2, 1).reshape(DOCS_DEV, cols * PI)


def per_device(layer_inputs, out_grads, doc_ids, proj_in, proj_out, query_feats):
    in_part = jnp.dot(layer_inputs, proj_in, preferred_element_type=jnp.float32)
    out_part = jnp.dot(out_grads, proj_out, preferred_element_type=jnp.float32)
    labels = doc_ids[0]
    width = lax.axis_size("tp")
    col_count = PO // width
    in_share, out_share = (
        lax.psum_scatter(in_part, "tp", scatter_dimension=0, tiled=True),
        lax.psum_scatter(out_part, "tp", scatter_dimension=0, tiled=True),
    )
    in_proj, out_proj = (
        lax.all_gather(in_share.astype(jnp.bfloat16), "tp", axis=0, tiled=True),
        lax.all_gather(out_share.astype(jnp.bfloat16), "tp", axis=0, tiled=True),
    )
    start = lax.axis_index("tp") * col_count
    out_cols = lax.dynamic_slice_in_dim(out_proj, start, col_count, 1)
    doc_feats = doc_features(labels, in_proj, out_cols).astype(jnp.bfloat16)
    mine = lax.psum_scatter(
        jnp.einsum("fq,ef->qe", query_feats, doc_feats, preferred_element_type=jnp.float32),
        "tp",
        scatter_dimension=0,
        tiled=True,
    )
    return mine.T


def solution(mesh):
    return jax.shard_map(
        per_device,
        mesh=mesh,
        in_specs=(
            P(("grp", "dp"), "tp"),
            P(("grp", "dp"), "tp"),
            P(("grp", "dp"), None),
            P("tp", None),
            P("tp", None),
            P("tp", None),
        ),
        out_specs=P(("grp", "dp"), "tp"),
        check_vma=False,
    )
```

profile of v0, /device:TPU:0, one launch (start us, length us, event | category | flops | bytes accessed | tf_op | source)
XLA Modules:
  0.0 103.5 jit_solution(4821030381208656163)
XLA Ops:
  6.5 0.0 copy-start
  6.5 0.0 copy-start.1
  6.5 0.0 reduce-scatter.4.cloned.1.call-start
  6.5 7.0 %fusion.15 = f32[2048,64]{0,1:T(8,128)} fusion(bf16[2048,2048]{1,0:T(8,128)(2,1)} %param.6, bf16[2048,64]{0,1:T(8,128)(2,1)} %param.9), kind=kOutput, calls=%fused_computation.13 | convolution fusion | flops 536870912 | bytes 9175040 | tf_op jit(solution)/shard_map/dot_general | solution.py:22
  13.5 0.0 reduce-scatter.4.cloned.1.call-update
  13.5 0.0 copy-start.2
  13.6 0.0 reduce-scatter.6.cloned.1.call-start
  13.6 0.0 copy-done.1
  13.6 15.0 %fusion.16 = f32[2048,64]{0,1:T(8,128)} fusion(bf16[2048,7168]{1,0:T(8,128)(2,1)} %param.7, bf16[7168,64]{0,1:T(8,128)(2,1)S(1)} %copy-done.1), kind=kOutput, calls=%fused_computation.14 | convolution fusion | flops 1879048192 | bytes 30801920 | tf_op jit(solution)/shard_map/dot_general | solution.py:23
  28.6 0.0 reduce-scatter.6.cloned.1.call-update
  28.6 0.0 reduce-scatter.8.cloned.1.call-start
  28.7 0.0 copy-done.2
  28.7 9.3 %reduce-scatter.4.cloned.1.call-done = f32[512,64]{0,1:T(8,128)} async-done(((f32[2048,64]{0,1:T(8,128)}), f32[512,64]{0,1:T(8,128)}) %reduce-scatter.4.cloned.1.call-update) | async-done | bytes 131088 | tf_op jit(solution)/shard_map/reduce_scatter | solution.py:28
  38.0 0.9 convert_element_type.23
  39.0 15.2 %all_gather.6 = bf16[2048,64]{0,1:T(8,128)(2,1)S(1)} all-gather(bf16[512,64]{0,1:T(8,128)(2,1)S(1)} %convert_element_type.23), channel_id=1, replica_groups=mesh['grp'=2,'tp'=4,'dp'=4] {'tp'}, dimensions={0}, use_global_device_ids=true | all-gather | bytes 327680 | tf_op jit(solution)/shard_map/all_gather | solution.py:32
  54.2 5.9 %reduce-scatter.6.cloned.1.call-done = f32[512,64]{0,1:T(8,128)} async-done(((f32[2048,64]{0,1:T(8,128)}), f32[512,64]{0,1:T(8,128)}) %reduce-scatter.6.cloned.1.call-update) | async-done | bytes 131088 | tf_op jit(solution)/shard_map/reduce_scatter | solution.py:29
  60.1 0.9 convert_element_type.24
  61.0 14.3 %all_gather.7 = bf16[2048,64]{0,1:T(8,128)(2,1)S(1)} all-gather(bf16[512,64]{0,1:T(8,128)(2,1)S(1)} %convert_element_type.24), channel_id=1, replica_groups=mesh['grp'=2,'tp'=4,'dp'=4] {'tp'}, dimensions={0}, use_global_device_ids=true | all-gather | bytes 327680 | tf_op jit(solution)/shard_map/all_gather | solution.py:33
  75.3 1.7 %fusion.8 = bf16[16,16,64]{2,1,0:T(8,128)(2,1)S(1)} fusion(bf16[2048,64]{0,1:T(8,128)(2,1)S(1)} %all_gather.6, bf16[2048,16]{0,1:T(8,128)(2,1)S(1)} %fusion.11, bf16[2048,64]{0,1:T(8,128)(2,1)S(1)} %all_gather.7, s32[]{:T(128)S(6)} %select_n.3), kind=kOutput, calls=%fused_computation.7 | convolution fusion | flops 69222400 | bytes 425988 | tf_op jit(solution)/shard_map/tk,tj->kj/dot_general | solution.py:16
  77.0 0.1 convert_element_type.27
  77.2 0.0 copy-done
  77.2 1.0 convolution_bitcast_fusion
  78.2 0.0 reduce-scatter.8.cloned.1.call-update
  78.2 18.8 %reduce-scatter.8.cloned.1.call-done = f32[256,16]{0,1:T(8,128)} async-done(((f32[1024,16]{0,1:T(8,128)}), f32[256,16]{0,1:T(8,128)}) %reduce-scatter.8.cloned.1.call-update) | async-done | bytes 16400 | tf_op jit(solution)/shard_map/reduce_scatter | solution.py:38
  (1 shorter events, 0.0 us)
Async XLA Ops:
  6.5 70.6 %copy-start = (bf16[1024,1024]{1,0:T(8,128)(2,1)S(1)}, bf16[1024,1024]{1,0:T(8,128)(2,1)}, u32[]{:S(2)}) copy-start(bf16[1024,1024]{1,0:T(8,128)(2,1)} %param.11) | copy-start | bytes 6291460
  6.5 7.1 %copy-start.1 = (bf16[7168,64]{0,1:T(8,128)(2,1)S(1)}, bf16[7168,64]{0,1:T(8,128)(2,1)}, u32[]{:S(2)}) copy-start(bf16[7168,64]{0,1:T(8,128)(2,1)} %param.10) | copy-start | bytes 2752516
  6.5 31.5 %reduce-scatter.4.cloned.1.call-start = ((), (), s32[]{:S(2)}) async-start(), calls=%async_computation.3 | async-start | bytes 655360 | tf_op jit(solution)/shard_map/reduce_scatter | solution.py:28
  13.5 15.1 %copy-start.2 = (s32[1,2048]{1,0:T(1,128)S(1)}, s32[1,2048]{1,0:T(1,128)}, u32[]{:S(2)}) copy-start(s32[1,2048]{1,0:T(1,128)} %param.8) | copy-start | bytes 24580
  13.6 46.5 %reduce-scatter.6.cloned.1.call-start = ((), (), s32[]{:S(2)}) async-start(), calls=%async_computation.4 | async-start | bytes 655360 | tf_op jit(solution)/shard_map/reduce_scatter | solution.py:29
  28.6 68.4 %reduce-scatter.8.cloned.1.call-start = ((), (), s32[]{:S(2)}) async-start(), calls=%async_computation.5 | async-start | bytes 81920 | tf_op jit(solution)/shard_map/reduce_scatter | solution.py:38
Sparse Core Ops, SparseCore 0:
  13.7 24.3 reduce-scatter.3
  40.3 19.7 reduce-scatter.5
  78.3 18.6 reduce-scatter.7
where the time goes:
time: 104 us
  waiting for transfers between devices  34 us (33%)
  blocking collectives  29.5 us (28%)
  matrix products  24.7 us (24%)
  between operations  13.2 us (13%)
  other arithmetic  1.84 us (2%)
    reduce_scatter x1, waiting for transfers between devices, per_device(): lax.psum_scatter(jnp.einsum('fq,ef->qe', query_feats, doc_feats, preferre...  18.8 us
    all_gather x1, blocking collectives, per_device(): lax.all_gather(in_share.astype(jnp.bfloat16), 'tp', axis=0, tiled=True)  15.2 us
    dot_general x1, matrix products, per_device(): out_part = jnp.dot(out_grads, proj_out, preferred_element_type=jnp.float32)  15 us
    all_gather x1, blocking collectives, per_device(): lax.all_gather(out_share.astype(jnp.bfloat16), 'tp', axis=0, tiled=True)  14.3 us
    reduce_scatter x1, waiting for transfers between devices, per_device(): lax.psum_scatter(in_part, 'tp', scatter_dimension=0, tiled=True)  9.31 us
    dot_general x1, matrix products, per_device(): in_part = jnp.dot(layer_inputs, proj_in, preferred_element_type=jnp.float32)  6.98 us
    reduce_scatter x1, waiting for transfers between devices, per_device(): lax.psum_scatter(out_part, 'tp', scatter_dimension=0, tiled=True)  5.88 us
  transfers between devices with their start and end apart: 3, of which 3 were waited for; matrix products, arithmetic and copies ran while one was open for 15% of the time, Pallas kernels for 0%

commit v1 on v0

v1 whole, which is shorter than its diff:
```python
import functools

import jax
import jax.numpy as jnp
from jax import lax
from jax.experimental import pallas as pl
from jax.experimental.pallas import tpu as pltpu
from jax.sharding import PartitionSpec as P

PI = 64
PO = 64
DOCS_DEV = 16
MESH = pl.DeviceIdType.MESH
BLOCK = 128


def kernel(
    n, block,
    x_hbm, g_hbm, ids_hbm, wi_hbm, wo_hbm, q_hbm, o_ref,
    x, g, ids, wi, wo, q, part, own, part_in, out_t, feat, feat_in, score, score_in,
    load_sem, const_sem, part_send, part_recv, feat_send, feat_recv, score_send, score_recv,
):
    tokens = x.shape[0]
    share = tokens // n
    chunks = share // block
    far = (n - 1) * chunks
    cols = PO // n
    me = lax.axis_index("tp")

    def peer(k):
        return lax.rem(me + 1 + k, n)

    barrier = pltpu.get_barrier_semaphore()
    for k in range(n - 1):
        pl.semaphore_signal(barrier, inc=1, device_id={"tp": peer(k)}, device_id_type=MESH)

    def rows(step):
        k, c = step // chunks, step % chunks
        return pl.ds(pl.multiple_of(peer(k) * share + c * block, block), block)

    def load_x(step):
        at = rows(step)
        return pltpu.make_async_copy(x_hbm.at[at], x.at[at], load_sem.at[0, step])

    def load_g(step):
        at = rows(step)
        return pltpu.make_async_copy(g_hbm.at[at], g.at[at], load_sem.at[1, step])

    load_wi = pltpu.make_async_copy(wi_hbm, wi, const_sem.at[0])
    load_wo = pltpu.make_async_copy(wo_hbm, wo, const_sem.at[1])
    load_q = pltpu.make_async_copy(q_hbm, q, const_sem.at[2])
    load_ids = pltpu.make_async_copy(
        ids_hbm.at[:, pl.ds(pl.multiple_of(me * share, share), share)], ids, const_sem.at[3]
    )

    load_wi.start()
    load_x(0).start()
    load_wo.start()
    load_g(0).start()

    def start_loads(step, carry):
        load_x(step).start()
        load_g(step).start()
        return carry

    lax.fori_loop(1, n * chunks, start_loads, 0)
    load_ids.start()
    load_q.start()

    def project(step):
        at = rows(step)
        load_x(step).wait()
        in_part = jnp.dot(x[at, :], wi[...], preferred_element_type=jnp.float32)
        load_g(step).wait()
        out_part = jnp.dot(g[at, :], wo[...], preferred_element_type=jnp.float32)
        return jnp.concatenate([in_part, out_part], axis=1)

    def send_part(step):
        k, c = step // chunks, step % chunks
        here = pl.ds(pl.multiple_of(c * block, block), block)
        return pltpu.make_async_remote_copy(
            src_ref=part.at[k, here],
            dst_ref=part_in.at[k, here],
            send_sem=part_send.at[step],
            recv_sem=part_recv.at[step],
            device_id={"tp": peer(k)},
            device_id_type=MESH,
        )

    load_wi.wait()
    load_wo.wait()
    pl.semaphore_wait(barrier, n - 1)

    def far_step(step, carry):
        k, c = step // chunks, step % chunks
        here = pl.ds(pl.multiple_of(c * block, block), block)
        part[k, here, :] = project(step).astype(jnp.bfloat16)
        send_part(step).start()
        return carry

    lax.fori_loop(0, far, far_step, 0)

    def own_step(c, carry):
        here = pl.ds(pl.multiple_of(c * block, block), block)
        own[here, :] = project(far + c)
        return carry

    lax.fori_loop(0, chunks, own_step, 0)

    def drain(step, carry):
        copy = send_part(step)
        copy.wait_send()
        copy.wait_recv()
        return carry

    lax.fori_loop(0, far, drain, 0)

    total = own[...]
    for k in range(n - 1):
        total = total + part_in[k].astype(jnp.float32)
    both = total.astype(jnp.bfloat16).astype(jnp.float32)
    lane = lax.broadcasted_iota(jnp.int32, both.shape, 1)
    twice = jnp.where(lane < PI, both, pltpu.roll(both, PI, 1)).astype(jnp.bfloat16)
    flipped = both.T
    for d in range(n):
        out_t[d] = flipped[PI + d * cols:PI + (d + 1) * cols, :]

    load_ids.wait()
    docs = lax.broadcasted_iota(jnp.int32, (DOCS_DEV, share), 0)
    mask = ids[...] == docs

    def doc_features(d):
        mine = out_t[d]
        spread = jnp.concatenate(
            [jnp.where(mask, mine[j:j + 1, :], 0.0).astype(jnp.bfloat16) for j in range(cols)], axis=0
        )
        feats = jnp.dot(spread, twice, preferred_element_type=jnp.float32)
        half = lax.broadcasted_iota(jnp.int32, (DOCS_DEV, 2 * PI), 1) < PI
        return [
            jnp.where(
                half,
                feats[2 * jp * DOCS_DEV:(2 * jp + 1) * DOCS_DEV],
                feats[(2 * jp + 1) * DOCS_DEV:(2 * jp + 2) * DOCS_DEV],
            )
            for jp in range(cols // 2)
        ]

    def send_feat(k):
        return pltpu.make_async_remote_copy(
            src_ref=feat.at[k],
            dst_ref=feat_in.at[k],
            send_sem=feat_send.at[k],
            recv_sem=feat_recv.at[k],
            device_id={"tp": peer(k)},
            device_id_type=MESH,
        )

    for k in range(n - 1):
        for jp, rows_jp in enumerate(doc_features(peer(k))):
            feat[k, jp] = rows_jp.astype(jnp.bfloat16)
        send_feat(k).start()
    sums = doc_features(me)
    load_q.wait()
    for k in range(n - 1):
        send_feat(k).wait_recv()
        sums = [s + feat_in[k, jp].astype(jnp.float32) for jp, s in enumerate(sums)]
    left = jnp.concatenate([s.astype(jnp.bfloat16) for s in sums], axis=1)
    scores = jnp.dot(left, q[...], preferred_element_type=jnp.float32)
    width = scores.shape[1] // n
    for d in range(n):
        score[d] = scores[:, d * width:(d + 1) * width]

    def send_score(k):
        return pltpu.make_async_remote_copy(
            src_ref=score.at[peer(k)],
            dst_ref=score_in.at[k],
            send_sem=score_send.at[k],
            recv_sem=score_recv.at[k],
            device_id={"tp": peer(k)},
            device_id_type=MESH,
        )

    for k in range(n - 1):
        send_score(k).start()
    result = score[me]
    for k in range(n - 1):
        send_score(k).wait_recv()
        result = result + score_in[k]
    o_ref[...] = result
    for k in range(n - 1):
        send_feat(k).wait_send()
        send_score(k).wait_send()


def per_device(n, layer_inputs, out_grads, doc_ids, proj_in, proj_out, query_feats):
    tokens = layer_inputs.shape[0]
    share = tokens // n
    block = min(BLOCK, share)
    steps = tokens // block
    far = (n - 1) * (share // block)
    cols = PO // n
    queries = query_feats.shape[1]
    width = queries // n
    wide = PI + PO
    bf16, f32 = jnp.bfloat16, jnp.float32
    flops = 2 * tokens * (proj_in.size + proj_out.size)
    moved = 2 * (layer_inputs.size + out_grads.size + proj_in.size + proj_out.size + query_feats.size)
    return pl.pallas_call(
        functools.partial(kernel, n, block),
        out_shape=jax.ShapeDtypeStruct((DOCS_DEV, width), f32),
        in_specs=[pl.BlockSpec(memory_space=pl.ANY)] * 6,
        out_specs=pl.BlockSpec(memory_space=pltpu.VMEM),
        scratch_shapes=[
            pltpu.VMEM(layer_inputs.shape, bf16),
            pltpu.VMEM(out_grads.shape, bf16),
            pltpu.VMEM((1, share), jnp.int32),
            pltpu.VMEM(proj_in.shape, bf16),
            pltpu.VMEM(proj_out.shape, bf16),
            pltpu.VMEM(query_feats.shape, bf16),
            pltpu.VMEM((n - 1, share, wide), bf16),
            pltpu.VMEM((share, wide), f32),
            pltpu.VMEM((n - 1, share, wide), bf16),
            pltpu.VMEM((n, cols, share), f32),
            pltpu.VMEM((n - 1, cols // 2, DOCS_DEV, 2 * PI), bf16),
            pltpu.VMEM((n - 1, cols // 2, DOCS_DEV, 2 * PI), bf16),
            pltpu.VMEM((n, DOCS_DEV, width), f32),
            pltpu.VMEM((n - 1, DOCS_DEV, width), f32),
            pltpu.SemaphoreType.DMA((2, steps)),
            pltpu.SemaphoreType.DMA((4,)),
            pltpu.SemaphoreType.DMA((far,)),
            pltpu.SemaphoreType.DMA((far,)),
            pltpu.SemaphoreType.DMA((n - 1,)),
            pltpu.SemaphoreType.DMA((n - 1,)),
            pltpu.SemaphoreType.DMA((n - 1,)),
            pltpu.SemaphoreType.DMA((n - 1,)),
        ],
        compiler_params=pltpu.CompilerParams(
            collective_id=0, has_side_effects=True, vmem_limit_bytes=56 * 1024 * 1024
        ),
        cost_estimate=pl.CostEstimate(flops=flops, bytes_accessed=moved, transcendentals=0),
    )(layer_inputs, out_grads, doc_ids, proj_in, proj_out, query_feats)


def solution(mesh):
    return jax.shard_map(
        functools.partial(per_device, mesh.shape["tp"]),
        mesh=mesh,
        in_specs=(
            P(("grp", "dp"), "tp"),
            P(("grp", "dp"), "tp"),
            P(("grp", "dp"), None),
            P("tp", None),
            P("tp", None),
            P("tp", None),
        ),
        out_specs=P(("grp", "dp"), "tp"),
        check_vma=False,
    )
```

time: 104 us -> 37.6 us (0.36)
  waiting for transfers between devices: 34 us -> 0 us
  Pallas kernels: 0 us -> 31.4 us
  blocking collectives: 29.5 us -> 0 us
  matrix products: 24.7 us -> 0 us
  between operations: 13.2 us -> 0.01 us
  local copies, waits for them, and re-layouts: 0.14 us -> 5.92 us
  other arithmetic: 1.84 us -> 0 us
    reduce_scatter x3 -> x0, waiting for transfers between devices: 34 us -> none  [the longest x1 18.8 us: per_device(): lax.psum_scatter(jnp.einsum('fq,ef->qe', query_feats, doc_feats, preferre...]
    pallas_call x0 -> x1, Pallas kernels: none -> 31.4 us  [per_device(): pl.pallas_call(functools.partial(kernel, n, block), out_shape=jax.ShapeDt...]
    all_gather x2 -> x0, blocking collectives: 29.5 us -> none  [the longest x1 15.2 us: per_device(): lax.all_gather(in_share.astype(jnp.bfloat16), 'tp', axis=0, tiled=True)]
    dot_general x4 -> x0, matrix products: 24.7 us -> none  [the longest x1 15 us: per_device(): out_part = jnp.dot(out_grads, proj_out, preferred_element_type=jnp.float32)]
    unnamed x6 -> x3, local copies, waits for them, and re-layouts: 0.01 us -> 5.92 us
    convert_element_type x3 -> x0, other arithmetic: 1.84 us -> none  [the longest x1 0.91 us: per_device(): in_share.astype(jnp.bfloat16)]
  transfers between devices with their start and end apart: 3 -> 0, of which waited for: 3 -> 0; matrix products, arithmetic and copies ran while one was open for 15% -> 0% of each run, Pallas kernels for 0% -> 0%
where the time goes in v1:
time: 37.6 us; the launch traced here: 37.4 us
  Pallas kernels  31.4 us (84%)
  local copies, waits for them, and re-layouts  5.92 us (16%)
    pallas_call x1, Pallas kernels, per_device(): pl.pallas_call(functools.partial(kernel, n, block), out_shape=jax.ShapeDt...  31.4 us
    unnamed x3, local copies, waits for them, and re-layouts  5.92 us

profile of v1, /device:TPU:0, one launch (start us, length us, event | category | flops | bytes accessed | tf_op | source)
XLA Modules:
  0.0 37.4 jit_solution(2871565962638863621)
XLA Ops:
  0.0 2.0 %copy.7.wi_hbm = bf16[2048,64]{1,0:T(8,128)(2,1)} copy(bf16[2048,64]{0,1:T(8,128)(2,1)} %param.9) | data formatting | bytes 524288 | tf_op args[3]
  2.0 2.6 %copy.8.wo_hbm = bf16[7168,64]{1,0:T(8,128)(2,1)} copy(bf16[7168,64]{0,1:T(8,128)(2,1)} %param.10) | data formatting | bytes 1835008 | tf_op args[4]
  4.6 31.4 %shard_map.64 = f32[16,256]{1,0:T(8,128)} custom-call(bf16[2048,2048]{1,0:T(8,128)(2,1)} %x_hbm.1, bf16[2048,7168]{1,0:T(8,128)(2,1)} %g_hbm.1, s32[1,2048]{1,0:T(1,128)} %ids_hbm.1, bf16[2048,64]{1,0:T(8,128)(2,1)} %copy.7.wi_hbm, bf16[7168,64]{1,0:T(8,128)(2,1)} %copy.8.wo_hbm, bf16[1024,1024]{1,0:T(8,128)(2,1)} %q_hbm.1), custom_call_target="tpu_custom_call" | custom-call | flops 2415919104 | bytes 41025536 | tf_op jit(solution)/shard_map/pallas_call | solution.py:208
  36.0 1.3 %copy.10 = f32[16,256]{1,0:T(8,128)} copy(f32[16,256]{1,0:T(8,128)} %shard_map.64) | data formatting | bytes 32768

commit v2 on v1

v2 whole, which is shorter than its diff:
```python
import functools

import jax
import jax.numpy as jnp
from jax import lax
from jax.experimental import pallas as pl
from jax.experimental.pallas import tpu as pltpu
from jax.sharding import PartitionSpec as P

PI = 64
PO = 64
DOCS_DEV = 16
MESH = pl.DeviceIdType.MESH
CHUNK = 7168


def across(a, b):
    return lax.dot_general(a, b, (((1,), (1,)), ((), ())), preferred_element_type=jnp.float32)


def chunks_of(width):
    chunk = CHUNK if width % CHUNK == 0 else width
    return [pl.ds(i, chunk) for i in range(0, width, chunk)]


def kernel(
    n,
    x_hbm, g_hbm, ids_hbm, wi_hbm, wo_hbm, q_hbm, o_ref,
    x, g, ids, wi, wo, q, part, own, part_in, out_t, feat, feat_in, score, score_out, score_in,
    load_sem, const_sem, part_send, part_recv, feat_send, feat_recv, score_send, score_recv,
):
    share = x.shape[0] // n
    cols = PO // n
    half_way = n // 2
    me = lax.axis_index("tp")
    pieces = [(x_hbm, x, wi, at) for at in chunks_of(x.shape[1])]
    pieces += [(g_hbm, g, wo, at) for at in chunks_of(g.shape[1])]

    def peer(k):
        away = k + k // half_way + (1 - (k + n - 1) // n) * half_way
        return lax.rem(me + away, n)

    barrier = pltpu.get_barrier_semaphore()
    for k in range(n - 1):
        pl.semaphore_signal(barrier, inc=1, device_id={"tp": peer(k)}, device_id_type=MESH)

    def rows(k):
        return pl.ds(pl.multiple_of(peer(k) * share, share), share)

    def load(k, i):
        source, target, _, at = pieces[i]
        return pltpu.make_async_copy(source.at[rows(k), at], target.at[rows(k), at], load_sem.at[i, k])

    load_wi = pltpu.make_async_copy(wi_hbm, wi, const_sem.at[0])
    load_wo = pltpu.make_async_copy(wo_hbm, wo, const_sem.at[1])
    load_q = pltpu.make_async_copy(q_hbm, q, const_sem.at[2])
    load_ids = pltpu.make_async_copy(
        ids_hbm.at[:, pl.ds(pl.multiple_of(me * share, share), share)], ids, const_sem.at[3]
    )

    load_wi.start()
    load(0, 0).start()
    load_wo.start()
    for i in range(1, len(pieces)):
        load(0, i).start()

    def start_loads(k, carry):
        for i in range(len(pieces)):
            load(k, i).start()
        return carry

    lax.fori_loop(1, n, start_loads, 0)
    load_ids.start()
    load_q.start()

    def send_part(k, side):
        return pltpu.make_async_remote_copy(
            src_ref=part.at[k, side],
            dst_ref=part_in.at[k, side],
            send_sem=part_send.at[side, k],
            recv_sem=part_recv.at[side, k],
            device_id={"tp": peer(k)},
            device_id_type=MESH,
        )

    load_wi.wait()
    load_wo.wait()
    pl.semaphore_wait(barrier, n - 1)

    def project(k, carry):
        for side, weight in enumerate((wi, wo)):
            done = 0.0
            for i, (_, data, held, at) in enumerate(pieces):
                if held is weight:
                    load(k, i).wait()
                    done = done + across(weight[:, at], data[rows(k), at])
            own[side] = done

            @pl.when(k < n - 1)
            def _():
                part[k, side] = done.astype(jnp.bfloat16)
                send_part(k, side).start()

        return carry

    lax.fori_loop(0, n, project, 0)

    total = own[...]
    for k in range(n - 1):
        send_part(k, 0).wait_recv()
        send_part(k, 1).wait_recv()
        total = total + part_in[k].astype(jnp.float32)
    high = total[0].astype(jnp.bfloat16)
    low = (total[0] - high.astype(jnp.float32)).astype(jnp.bfloat16)
    twice = jnp.concatenate([high, high, low, low], axis=0)
    flipped = total[1].astype(jnp.bfloat16).astype(jnp.float32)
    for d in range(n):
        out_t[d] = flipped[d * cols:(d + 1) * cols, :]

    load_ids.wait()
    docs = lax.broadcasted_iota(jnp.int32, (DOCS_DEV, share), 0)
    mask = ids[...] == docs

    def doc_features(d):
        mine = out_t[d]
        spread = jnp.concatenate(
            [jnp.where(mask, mine[j:j + 1, :], 0.0).astype(jnp.bfloat16) for j in range(cols)], axis=0
        )
        feats = across(spread, twice)
        feats = feats[:, :2 * PI] + feats[:, 2 * PI:]
        half = lax.broadcasted_iota(jnp.int32, (DOCS_DEV, 2 * PI), 1) < PI
        return [
            jnp.where(
                half,
                feats[2 * jp * DOCS_DEV:(2 * jp + 1) * DOCS_DEV],
                feats[(2 * jp + 1) * DOCS_DEV:(2 * jp + 2) * DOCS_DEV],
            )
            for jp in range(cols // 2)
        ]

    def send_feat(k):
        return pltpu.make_async_remote_copy(
            src_ref=feat.at[k],
            dst_ref=feat_in.at[k],
            send_sem=feat_send.at[k],
            recv_sem=feat_recv.at[k],
            device_id={"tp": peer(k)},
            device_id_type=MESH,
        )

    for k in range(n - 1):
        for jp, rows_jp in enumerate(doc_features(peer(k))):
            feat[k, jp] = rows_jp.astype(jnp.bfloat16)
        send_feat(k).start()
    sums = doc_features(me)
    load_q.wait()
    for k in range(n - 1):
        send_feat(k).wait_recv()
        sums = [s + feat_in[k, jp].astype(jnp.float32) for jp, s in enumerate(sums)]
    left = jnp.concatenate(sums, axis=1)
    high = left.astype(jnp.bfloat16)
    low = (left - high.astype(jnp.float32)).astype(jnp.bfloat16)
    scores = jnp.dot(jnp.concatenate([high, low], axis=0), q[...], preferred_element_type=jnp.float32)
    scores = scores[:DOCS_DEV] + scores[DOCS_DEV:]
    width = scores.shape[1] // n
    for d in range(n):
        score[d] = scores[:, d * width:(d + 1) * width]
        score_out[d] = score[d].astype(jnp.bfloat16)

    def send_score(k):
        return pltpu.make_async_remote_copy(
            src_ref=score_out.at[peer(k)],
            dst_ref=score_in.at[k],
            send_sem=score_send.at[k],
            recv_sem=score_recv.at[k],
            device_id={"tp": peer(k)},
            device_id_type=MESH,
        )

    for k in range(n - 1):
        send_score(k).start()
    result = score[me]
    for k in range(n - 1):
        send_score(k).wait_recv()
        result = result + score_in[k].astype(jnp.float32)
    o_ref[...] = result
    for k in range(n - 1):
        send_part(k, 0).wait_send()
        send_part(k, 1).wait_send()
        send_feat(k).wait_send()
        send_score(k).wait_send()


def per_device(n, layer_inputs, out_grads, doc_ids, proj_in, proj_out, query_feats):
    tokens = layer_inputs.shape[0]
    share = tokens // n
    loads = len(chunks_of(layer_inputs.shape[1])) + len(chunks_of(out_grads.shape[1]))
    cols = PO // n
    queries = query_feats.shape[1]
    width = queries // n
    bf16, f32 = jnp.bfloat16, jnp.float32
    flops = 2 * tokens * (proj_in.size + proj_out.size)
    moved = 2 * (layer_inputs.size + out_grads.size + proj_in.size + proj_out.size + query_feats.size)
    return pl.pallas_call(
        functools.partial(kernel, n),
        out_shape=jax.ShapeDtypeStruct((DOCS_DEV, width), f32),
        in_specs=[pl.BlockSpec(memory_space=pl.ANY)] * 6,
        out_specs=pl.BlockSpec(memory_space=pltpu.VMEM),
        scratch_shapes=[
            pltpu.VMEM(layer_inputs.shape, bf16),
            pltpu.VMEM(out_grads.shape, bf16),
            pltpu.VMEM((1, share), jnp.int32),
            pltpu.VMEM(proj_in.shape[::-1], bf16),
            pltpu.VMEM(proj_out.shape[::-1], bf16),
            pltpu.VMEM(query_feats.shape, bf16),
            pltpu.VMEM((n - 1, 2, PI, share), bf16),
            pltpu.VMEM((2, PI, share), f32),
            pltpu.VMEM((n - 1, 2, PI, share), bf16),
            pltpu.VMEM((n, cols, share), f32),
            pltpu.VMEM((n - 1, cols // 2, DOCS_DEV, 2 * PI), bf16),
            pltpu.VMEM((n - 1, cols // 2, DOCS_DEV, 2 * PI), bf16),
            pltpu.VMEM((n, DOCS_DEV, width), f32),
            pltpu.VMEM((n, DOCS_DEV, width), bf16),
            pltpu.VMEM((n - 1, DOCS_DEV, width), bf16),
            pltpu.SemaphoreType.DMA((loads, n)),
            pltpu.SemaphoreType.DMA((4,)),
            pltpu.SemaphoreType.DMA((2, n - 1)),
            pltpu.SemaphoreType.DMA((2, n - 1)),
            pltpu.SemaphoreType.DMA((n - 1,)),
            pltpu.SemaphoreType.DMA((n - 1,)),
            pltpu.SemaphoreType.DMA((n - 1,)),
            pltpu.SemaphoreType.DMA((n - 1,)),
        ],
        compiler_params=pltpu.CompilerParams(
            collective_id=0, has_side_effects=True, vmem_limit_bytes=56 * 1024 * 1024
        ),
        cost_estimate=pl.CostEstimate(flops=flops, bytes_accessed=moved, transcendentals=0),
    )(layer_inputs, out_grads, doc_ids, proj_in.T, proj_out.T, query_feats)


def solution(mesh):
    return jax.shard_map(
        functools.partial(per_device, mesh.shape["tp"]),
        mesh=mesh,
        in_specs=(
            P(("grp", "dp"), "tp"),
            P(("grp", "dp"), "tp"),
            P(("grp", "dp"), None),
            P("tp", None),
            P("tp", None),
            P("tp", None),
        ),
        out_specs=P(("grp", "dp"), "tp"),
        check_vma=False,
    )
```

time: 37.6 us -> 31.1 us (0.83)
  local copies, waits for them, and re-layouts: 5.92 us -> 1.32 us
  Pallas kernels: 31.4 us -> 29.5 us
    unnamed x3 -> x1, local copies, waits for them, and re-layouts: 5.92 us -> 1.32 us
    pallas_call x1, Pallas kernels: 31.4 us -> 29.5 us  [per_device(): pl.pallas_call(functools.partial(kernel, n), out_shape=jax.ShapeDtypeStru...]
where the time goes in v2:
time: 31.1 us; the launch traced here: 30.9 us
  Pallas kernels  29.5 us (95%)
  local copies, waits for them, and re-layouts  1.32 us (4%)
    pallas_call x1, Pallas kernels, per_device(): pl.pallas_call(functools.partial(kernel, n), out_shape=jax.ShapeDtypeStru...  29.5 us
    unnamed x1, local copies, waits for them, and re-layouts  1.32 us

profile of v2, /device:TPU:0, one launch (start us, length us, event | category | flops | bytes accessed | tf_op | source)
XLA Modules:
  0.0 30.9 jit_solution(6265413695902660350)
XLA Ops:
  0.0 29.5 %shard_map.64 = f32[16,256]{1,0:T(8,128)} custom-call(bf16[2048,2048]{1,0:T(8,128)(2,1)} %x_hbm.1, bf16[2048,7168]{1,0:T(8,128)(2,1)} %g_hbm.1, s32[1,2048]{1,0:T(1,128)} %ids_hbm.1, bf16[64,2048]{1,0:T(8,128)(2,1)} %bitcast.3, bf16[64,7168]{1,0:T(8,128)(2,1)} %bitcast.2, bf16[1024,1024]{1,0:T(8,128)(2,1)} %q_hbm.1), custom_call_target="tpu_custom_call" | custom-call | flops 2415919104 | bytes 41025536 | tf_op jit(solution)/shard_map/pallas_call | solution.py:204
  29.5 1.3 %copy.8 = f32[16,256]{1,0:T(8,128)} copy(f32[16,256]{1,0:T(8,128)} %shard_map.64) | data formatting | bytes 32768

commit v3 on v2

--- a/solution.py
+++ b/solution.py
@@ -84,12 +84,17 @@
         )
 
     load_wi.wait()
-    load_wo.wait()
     pl.semaphore_wait(barrier, n - 1)
 
     def project(k, carry):
         for side, weight in enumerate((wi, wo)):
             done = 0.0
+            if side == 1:
+
+                @pl.when(k == 0)
+                def _():
+                    load_wo.wait()
+
             for i, (_, data, held, at) in enumerate(pieces):
                 if held is weight:
                     load(k, i).wait()

time: 31.1 us -> 31.1 us (level)
  no operation moved by 1% of the time
where the time goes in v3:
time: 31.1 us; the launch traced here: 30.9 us
  Pallas kernels  29.5 us (95%)
  local copies, waits for them, and re-layouts  1.32 us (4%)
    pallas_call x1, Pallas kernels, per_device(): pl.pallas_call(functools.partial(kernel, n), out_shape=jax.ShapeDtypeStru...  29.5 us
    unnamed x1, local copies, waits for them, and re-layouts  1.32 us

profile of v3, /device:TPU:0, one launch (start us, length us, event | category | flops | bytes accessed | tf_op | source)
XLA Modules:
  0.0 30.9 jit_solution(9104826082473599240)
XLA Ops:
  0.0 29.5 %shard_map.64 = f32[16,256]{1,0:T(8,128)} custom-call(bf16[2048,2048]{1,0:T(8,128)(2,1)} %x_hbm.1, bf16[2048,7168]{1,0:T(8,128)(2,1)} %g_hbm.1, s32[1,2048]{1,0:T(1,128)} %ids_hbm.1, bf16[64,2048]{1,0:T(8,128)(2,1)} %bitcast.3, bf16[64,7168]{1,0:T(8,128)(2,1)} %bitcast.2, bf16[1024,1024]{1,0:T(8,128)(2,1)} %q_hbm.1), custom_call_target="tpu_custom_call" | custom-call | flops 2415919104 | bytes 41025536 | tf_op jit(solution)/shard_map/pallas_call | solution.py:209
  29.5 1.3 %copy.8 = f32[16,256]{1,0:T(8,128)} copy(f32[16,256]{1,0:T(8,128)} %shard_map.64) | data formatting | bytes 32768
